TPU v7x, 512 devices: a whole 4x4x16 slice. The times are simulated.
512 devices in a mesh: grp: 16 (over y_lo, x, core), slab: 32 (over z, y_hi).
Axes of the slice: x: 4, y: 4 (y_hi: 2, y_lo: 2; y = y_hi * 2 + y_lo), z: 16, core: 2. Of those that a mesh axis runs over, the one named last changes fastest.
Arguments:
- amplitudes: float32 [4096, 65536], P('grp', 'slab'), may hold values from -6 to 6, as said below
- ladder_ints: float32 [65536, 1024], P('slab', 'grp'), may hold values from -1 to 1, as said below
- cycle_ints: float32 [16384, 512], P('grp'), may hold values from -1 to 1, as said below
- occ_irrep: int32 [64], replicated, may hold values from 0 to 7, as said below
- vir_irrep: int32 [256], replicated, may hold values from 0 to 7, as said below
Outputs:
- ladder_term: float32 [4096, 1024], P('grp', 'slab')
- cycle_term: float32 [64, 256, 512], P('grp', 'slab')
Inputs may be any that keep to these rules, and one draw needn't show every extreme that they name: `occ_irrep`: nondecreasing: the occupied orbitals are ordered by irrep. `vir_irrep`: nondecreasing: the virtual orbitals are ordered by irrep. amplitudes[i * 64 + j, a * 256 + b] is zero unless xor(occ_irrep[i], occ_irrep[j]) equals xor(vir_irrep[a], vir_irrep[b]). ladder_ints[c * 256 + d, a * 256 + b] is zero unless xor(vir_irrep[c], vir_irrep[d]) equals xor(vir_irrep[a], vir_irrep[b]). cycle_ints[k * 256 + c, j * 256 + b] is zero unless xor(occ_irrep[k], vir_irrep[c]) equals xor(occ_irrep[j], vir_irrep[b]).
All inputs are finite; a program needn't handle non-finite values.
Results may differ from a plain program's by a relative error of at most 0.000077.
Values sent between devices are 32-bit elements; how exact they have to be, the bound alone decides.
A program may use at most 64 MiB of HBM per device.

v0:
```python
import jax
import jax.numpy as jnp
from jax import lax
from jax.sharding import PartitionSpec as P


def allowed_mask(lab_i, lab_j, lab_a, lab_b):
    left = jnp.bitwise_xor(lab_i, lab_j)
    right = jnp.bitwise_xor(lab_a, lab_b)
    return left == right


def per_device(amplitudes, ladder_ints, cycle_ints, occ_irrep, vir_irrep):
    groups = lax.axis_size("grp")
    slabs = lax.axis_size("slab")
    grp_index = lax.axis_index("grp")
    slab_index = lax.axis_index("slab")
    occ_count = occ_irrep.shape[0]
    vir_count = vir_irrep.shape[0]
    occ_local = amplitudes.shape[0] // occ_count
    vir_local = amplitudes.shape[1] // vir_count
    window = ladder_ints.shape[1] * groups
    ladder_cols = window // slabs
    a_count = window // vir_count
    partial_sum = jnp.dot(
        amplitudes,
        lax.all_gather(ladder_ints, "grp", axis=1, tiled=True),
        precision=lax.Precision.HIGHEST,
        preferred_element_type=jnp.float32,
    )
    ladder = lax.psum_scatter(partial_sum, "slab", scatter_dimension=1, tiled=True)
    occ_mine = lax.dynamic_slice_in_dim(occ_irrep, grp_index * occ_local, occ_local, 0)
    row_i = jnp.repeat(occ_mine, occ_count)
    row_j = jnp.tile(occ_irrep, occ_local)
    col_a = lax.dynamic_slice_in_dim(
        jnp.repeat(vir_irrep[:a_count], vir_count), slab_index * ladder_cols, ladder_cols, 0
    )
    col_b = lax.dynamic_slice_in_dim(
        jnp.tile(vir_irrep, a_count), slab_index * ladder_cols, ladder_cols, 0
    )
    ladder_keep = allowed_mask(row_i[:, None], row_j[:, None], col_a[None, :], col_b[None, :])
    ladder_term = jnp.where(ladder_keep, ladder, jnp.float32(0.0))
    blocks = amplitudes.reshape(occ_local, occ_count, vir_local, vir_count)
    k_local = cycle_ints.shape[0] // vir_count
    cycle_cols = cycle_ints.shape[1]
    cycle_table = cycle_ints.reshape(k_local, vir_count, cycle_cols)
    regrouped = lax.all_to_all(blocks, "grp", split_axis=1, concat_axis=0, tiled=True)
    partial_cycle = jnp.einsum(
        "ikac,kcw->iaw", regrouped, cycle_table, precision=lax.Precision.HIGHEST
    )
    cycle = lax.psum_scatter(partial_cycle, "grp", scatter_dimension=0, tiled=True)
    j_count = cycle_cols // vir_count
    vir_mine = lax.dynamic_slice_in_dim(vir_irrep, slab_index * vir_local, vir_local, 0)
    col_j = jnp.repeat(occ_irrep[:j_count], vir_count)
    col_jb = jnp.tile(vir_irrep, j_count)
    cycle_keep = allowed_mask(
        occ_mine[:, None, None],
        col_j[None, None, :],
        vir_mine[None, :, None],
        col_jb[None, None, :],
    )
    cycle_term = jnp.where(cycle_keep, cycle, jnp.float32(0.0))
    return (ladder_term, cycle_term)


def solution(mesh):
    return jax.shard_map(
        per_device,
        mesh=mesh,
        in_specs=(P("grp", "slab"), P("slab", "grp"), P("grp", None), P(), P()),
        out_specs=(P("grp", "slab"), P("grp", "slab", None)),
        check_vma=False,
    )
```

profile of v0, /device:TPU:6, one launch (start us, length us, event | category | flops | bytes accessed | tf_op | source)
XLA Modules:
  0.0 831.2 jit_solution(3712130718410636174)
XLA Ops:
  7.2 0.0 copy-start
  7.2 0.0 all-gather.2.cloned.1.call-start
  7.2 0.7 all-gather.2.cloned.1.call-update
  7.9 0.0 reduce-scatter.5.cloned.1.call-start
  8.0 2.5 copy.19
  10.4 0.3 copy.10
  10.7 44.1 %all_to_all.18 = f32[4,64,8,256]{3,2,0,1:T(8,128)S(1)} all-to-all(f32[4,64,8,256]{3,2,0,1:T(8,128)S(1)} %copy.10), channel_id=1, replica_groups=mesh['grp'=16,'slab'=32] {'grp'}, dimensions={1} | all-to-all | bytes 4194304 | tf_op jit(solution)/shard_map/all_to_all | solution.py:47
  54.8 0.3 copy.12
  55.1 0.0 copy-done
  55.1 4.5 convolution_bitcast_fusion
  59.6 0.0 reduce-scatter.5.cloned.1.call-update
  59.6 0.0 copy-start.2
  59.6 0.0 copy-start.1
  59.7 0.0 slice-start
  59.7 0.0 reduce-scatter.3.cloned.1.call-start
  59.7 25.5 %all-gather.2.cloned.1.call-done = f32[2048,1024]{0,1:T(8,128)} async-done(((f32[2048,64]{0,1:T(8,128)}), f32[2048,1024]{0,1:T(8,128)}) %all-gather.2.cloned.1.call-update) | async-done | bytes 8388624 | tf_op jit(solution)/shard_map/all_gather | solution.py:27
  85.2 10.6 %fusion = f32[256,1024]{0,1:T(8,128)} fusion(f32[256,2048]{1,0:T(8,128)} %param.5, f32[2048,1024]{0,1:T(8,128)} %all-gather.2.cloned.1.call-done), kind=kOutput, calls=%fused_computation.11 | convolution fusion | flops 6442450944 | bytes 11534336 | tf_op jit(solution)/shard_map/dot_general | solution.py:25
  95.9 0.0 reduce-scatter.3.cloned.1.call-update
  95.9 0.0 copy-done.2
  95.9 0.1 dynamic_slice.12
  96.0 0.1 broadcast_xor_fusion.2
  96.0 0.1 xor.56
  96.2 0.1 broadcast_bitcast_fusion.1
  96.2 0.1 dynamic_slice.15
  96.3 0.1 broadcast_bitcast_fusion.3
  96.4 0.1 dynamic-slice_xor_fusion
  96.5 0.1 broadcast_xor_fusion.1
  96.5 0.1 broadcast_xor_fusion
  96.6 57.8 %reduce-scatter.5.cloned.1.call-done = f32[4,8,512]{2,1,0:T(8,128)} async-done(((f32[64,8,512]{2,1,0:T(8,128)}), f32[4,8,512]{2,1,0:T(8,128)}) %reduce-scatter.5.cloned.1.call-update) | async-done | bytes 65552 | tf_op jit(solution)/shard_map/reduce_scatter | solution.py:51
  154.4 1.5 compare_select_fusion
  155.9 667.3 %reduce-scatter.3.cloned.1.call-done = f32[256,32]{0,1:T(8,128)} async-done(((f32[256,1024]{0,1:T(8,128)}), f32[256,32]{0,1:T(8,128)}) %reduce-scatter.3.cloned.1.call-update) | async-done | bytes 32784 | tf_op jit(solution)/shard_map/reduce_scatter | solution.py:31
  823.2 1.4 compare_select_fusion.1
  (8 shorter events, 0.0 us)
Async XLA Ops:
  7.2 47.9 %copy-start = (f32[1024,512]{1,0:T(8,128)S(1)}, f32[1024,512]{1,0:T(8,128)}, u32[]{:S(2)}) copy-start(f32[1024,512]{1,0:T(8,128)} %param.7) | copy-start | bytes 6291460
  7.2 78.0 %all-gather.2.cloned.1.call-start = ((), (), s32[]{:S(2)}) async-start(), calls=%async_computation.3 | async-start | bytes 8912896 | tf_op jit(solution)/shard_map/all_gather | solution.py:27
  7.9 146.5 %reduce-scatter.5.cloned.1.call-start = ((), (), s32[]{:S(2)}) async-start(), calls=%async_computation.5 | async-start | bytes 1114112 | tf_op jit(solution)/shard_map/reduce_scatter | solution.py:51
  59.6 36.3 %copy-start.2 = (s32[64]{0:T(128)S(1)}, s32[64]{0:T(128)}, u32[]{:S(2)}) copy-start(s32[64]{0:T(128)} %param.8) | copy-start | bytes 772
  59.6 36.5 %copy-start.1 = (s32[256]{0:T(256)S(1)}, s32[256]{0:T(256)}, u32[]{:S(2)}) copy-start(s32[256]{0:T(256)} %param.9) | copy-start | bytes 3076
  59.7 36.5 %slice-start = ((s32[256]{0:T(256)}), s32[4]{0:T(128)S(1)}, s32[]{:S(2)}) async-start(s32[256]{0:T(256)} %param.9), calls=%async_computation.6 | async-start | bytes 1024 | tf_op jit(solution)/shard_map/slice | solution.py:36
  59.7 763.5 %reduce-scatter.3.cloned.1.call-start = ((), (), s32[]{:S(2)}) async-start(), calls=%async_computation.4 | async-start | bytes 1081344 | tf_op jit(solution)/shard_map/reduce_scatter | solution.py:31
Sparse Core Ops, SparseCore 0:
  10.2 75.0 all-gather.1
  88.0 66.3 reduce-scatter.4
  159.4 663.7 reduce-scatter.2
where the time goes:
time: 831 us
  waiting for transfers between devices  751 us (90%)
  blocking collectives  44.1 us (5%)
  matrix products  15.1 us (2%)
  between operations  13.8 us (2%)
    reduce_scatter x1, waiting for transfers between devices, per_device(): lax.psum_scatter(partial_sum, 'slab', scatter_dimension=1, tiled=True)  667 us
    reduce_scatter x1, waiting for transfers between devices, per_device(): lax.psum_scatter(partial_cycle, 'grp', scatter_dimension=0, tiled=True)  57.8 us
    all_to_all x1, blocking collectives, per_device(): lax.all_to_all(blocks, 'grp', split_axis=1, concat_axis=0, tiled=True)  44.1 us
    all_gather x1, waiting for transfers between devices, per_device(): lax.all_gather(ladder_ints, 'grp', axis=1, tiled=True)  25.5 us
  transfers between devices with their start and end apart: 3, of which 3 were waited for; matrix products, arithmetic and copies ran while one was open for 2% of the time, Pallas kernels for 0%

commit v1 on v0

--- a/solution.py
+++ b/solution.py
@@ -1,7 +1,16 @@
+import functools
+
 import jax
 import jax.numpy as jnp
 from jax import lax
+from jax.experimental import pallas as pl
+from jax.experimental.pallas import tpu as pltpu
 from jax.sharding import PartitionSpec as P
+
+FOLD = 64
+IRREPS = 8
+MESH = pl.DeviceIdType.MESH
+EXACT = lax.Precision.HIGHEST
 
 
 def allowed_mask(lab_i, lab_j, lab_a, lab_b):
@@ -10,7 +19,7 @@
     return left == right
 
 
-def per_device(amplitudes, ladder_ints, cycle_ints, occ_irrep, vir_irrep):
+def dense_path(amplitudes, ladder_ints, cycle_ints, occ_irrep, vir_irrep):
     groups = lax.axis_size("grp")
     slabs = lax.axis_size("slab")
     grp_index = lax.axis_index("grp")
@@ -63,6 +72,381 @@
     return (ladder_term, cycle_term)
 
 
+def folded_kernel(
+    starts, amp_hbm, lad_hbm, cyc_hbm, lad_out, cyc_out,
+    amp, lad, cyc, amp_fold, a2a_send, a2a_recv, cyc_fold, gath, rhs, zed, y_recv, z_send, z_recv, quad,
+    lhs, c_part, c_send, c_recv, c_full,
+    load_sem, g_ss, g_rs, a_ss, a_rs, y_ss, y_rs, z_ss, z_rs, q_ss, q_rs, c_ss, c_rs,
+):
+    f32, i32 = jnp.float32, jnp.int32
+    g, s = lax.axis_index("grp"), lax.axis_index("slab")
+    core, x, y = g % 2, (g // 2) % 4, g // 8
+    z, half = s // 2, s % 2
+
+    load_l = pltpu.make_async_copy(lad_hbm, lad, load_sem.at[0])
+    load_a = pltpu.make_async_copy(amp_hbm, amp, load_sem.at[1])
+    load_w = pltpu.make_async_copy(cyc_hbm, cyc, load_sem.at[2])
+    load_l.start()
+    load_a.start()
+    load_w.start()
+
+    barrier = pltpu.get_barrier_semaphore()
+
+    @pl.loop(1, 16)
+    def _(r):
+        pl.semaphore_signal(barrier, inc=1, device_id=((g + r) % 16, s), device_id_type=MESH)
+        pl.semaphore_signal(barrier, inc=1, device_id=(g, ((z + r) % 16) * 2 + half), device_id_type=MESH)
+
+    pl.semaphore_signal(barrier, inc=1, device_id=(g, z * 2 + (1 - half)), device_id_type=MESH)
+
+    def iota(shape, dim):
+        return lax.broadcasted_iota(i32, shape, dim)
+
+    def label(index, base):
+        total = jnp.where(index >= starts[base + 1], 1, 0)
+        for v in range(2, IRREPS):
+            total = total + jnp.where(index >= starts[base + v], 1, 0)
+        return total
+
+    occ_label = functools.partial(label, base=0)
+    vir_label = functools.partial(label, base=IRREPS)
+    low64 = iota((1, 128), 1) < 64
+
+    def pack_pair(first, second):
+        keep = jnp.where(low64, first, second)
+        move = jnp.where(low64, second, first)
+        return keep + pltpu.roll(move, 64, 1)
+
+    def swap_pair(first, second):
+        return (
+            jnp.where(low64, first, pltpu.roll(second, 64, 1)),
+            jnp.where(low64, pltpu.roll(first, 64, 1), second),
+        )
+
+    def regroup(src, dst, blocks):
+        low4 = iota((8, 1), 0) < 4
+
+        @pl.loop(0, 8)
+        def _(q):
+            for n in range(0, blocks, 2):
+                for c in range(src.shape[1] // 128):
+                    cols = slice(128 * c, 128 * c + 128)
+                    one = src[pl.ds(pl.multiple_of(64 * n + 8 * q, 8), 8), cols]
+                    two = src[pl.ds(pl.multiple_of(64 * n + 64 + 8 * q, 8), 8), cols]
+                    dst[2 * q, c, 4 * n : 4 * n + 8, :] = jnp.where(low4, one, pltpu.roll(two, 4, 0))
+                    dst[2 * q + 1, c, 4 * n : 4 * n + 8, :] = jnp.where(low4, pltpu.roll(one, 4, 0), two)
+
+    load_l.wait()
+
+    @pl.loop(0, 4)
+    def _(c):
+        parts = []
+        for c_half in range(2):
+            base = 256 * c + 1024 * c_half
+            part = lad[pl.ds(pl.multiple_of(base, 64), 64), :]
+            for m in range(1, 4):
+                part = part + lad[pl.ds(pl.multiple_of(base + 64 * m, 64), 64), :]
+            parts.append(part)
+        gath[g, pl.ds(pl.multiple_of(64 * c, 64), 64), :] = jnp.concatenate(parts, axis=1)
+
+    pl.semaphore_wait(barrier, 31)
+
+    def at(y_, x_, core_):
+        return (y_ * 4 + x_ % 4) * 2 + core_
+
+    sib, y_dev = at(y, x, 1 - core), at(1 - y, x, core)
+    right, left = at(y, x + 1, core), at(y, x + 3, core)
+    y_right, y_left = at(1 - y, x + 1, core), at(1 - y, x + 3, core)
+    across, y_across = at(y, x + 2, core), at(1 - y, x + 2, core)
+
+    def g_copy(k, slot, dev, rows=slice(None)):
+        ref = gath.at[slot] if rows == slice(None) else gath.at[slot, rows]
+        return pltpu.make_async_remote_copy(
+            src_ref=ref, dst_ref=ref, send_sem=g_ss.at[k], recv_sem=g_rs.at[k],
+            device_id=(dev, s), device_id_type=MESH,
+        )
+
+    lower, upper = pl.ds(0, 128), pl.ds(128, 128)
+    moves = [
+        g_copy(0, g, y_dev), g_copy(1, g, right), g_copy(2, g, left), g_copy(3, g, sib),
+        g_copy(4, y_dev, right), g_copy(5, y_dev, left), g_copy(6, y_dev, sib),
+        g_copy(7, left, right, lower), g_copy(8, right, left, upper),
+        g_copy(9, y_left, right, lower), g_copy(10, y_right, left, upper),
+        g_copy(11, left, sib), g_copy(12, right, sib), g_copy(13, y_left, sib), g_copy(14, y_right, sib),
+        g_copy(15, across, sib), g_copy(16, y_across, sib),
+    ]
+    for k in range(4):
+        moves[k].start()
+
+    load_a.wait()
+
+    @pl.loop(0, 16)
+    def _(r):
+        rows = pl.ds(pl.multiple_of(16 * r, 16), 16)
+        for m in range(4):
+            even = amp[rows, 512 * m : 512 * m + 128] + amp[rows, 512 * m + 128 : 512 * m + 256]
+            odd = amp[rows, 512 * m + 256 : 512 * m + 384] + amp[rows, 512 * m + 384 : 512 * m + 512]
+            amp_fold[rows, 128 * m : 128 * m + 128] = pack_pair(even, odd)
+
+    regroup(amp_fold, a2a_send, 4)
+    moves[0].wait_recv()
+    for k in range(4, 7):
+        moves[k].start()
+
+    def a_copy(r):
+        to = (g + r) % 16
+        return pltpu.make_async_remote_copy(
+            src_ref=a2a_send.at[to], dst_ref=a2a_recv.at[:, pl.ds(pl.multiple_of(16 * g, 16), 16)],
+            send_sem=a_ss.at[r], recv_sem=a_rs.at[r], device_id=(to, s), device_id_type=MESH,
+        )
+
+    a2a_recv[:, pl.ds(pl.multiple_of(16 * g, 16), 16), :] = a2a_send[g]
+
+    @pl.loop(1, 16)
+    def _(r):
+        a_copy(r).start()
+
+    moves[1].wait_recv()
+    moves[7].start()
+    moves[11].start()
+    moves[2].wait_recv()
+    moves[8].start()
+    moves[12].start()
+
+    load_w.wait()
+
+    @pl.loop(0, 4)
+    def _(k):
+        part = cyc[pl.ds(pl.multiple_of(256 * k, 64), 64), :]
+        for m in range(1, 4):
+            part = part + cyc[pl.ds(pl.multiple_of(256 * k + 64 * m, 64), 64), :]
+        cyc_fold[pl.ds(pl.multiple_of(64 * k, 64), 64), :] = part
+
+    moves[4].wait_recv()
+    moves[9].start()
+    moves[13].start()
+    moves[5].wait_recv()
+    moves[10].start()
+    moves[14].start()
+    moves[7].wait_recv()
+    moves[8].wait_recv()
+    moves[15].start()
+    moves[9].wait_recv()
+    moves[10].wait_recv()
+    moves[16].start()
+    for k in (3, 6, 11, 12, 13, 14, 15, 16):
+        moves[k].wait_recv()
+
+    lane = iota((1, 128), 1)
+    lane_block = lane // 32
+
+    def pair_label(i):
+        return occ_label(4 * g + i) ^ occ_label(iota((64, 128), 0))
+
+    row_label = jnp.concatenate([pair_label(i) for i in range(4)], axis=0)
+
+    @pl.loop(0, 4)
+    def _(a):
+        for pair in range(2):
+            low, high = swap_pair(gath[4 * a + 2 * pair], gath[4 * a + 2 * pair + 1])
+            rhs[0:256, 128 * pair : 128 * pair + 128] = low
+            rhs[256:512, 128 * pair : 128 * pair + 128] = high
+        product = jnp.dot(amp_fold[...], rhs[...], precision=EXACT, preferred_element_type=f32)
+        kept = [
+            jnp.where(
+                row_label == (vir_label(a) ^ vir_label(lane + 128 * part)),
+                product[:, 128 * part : 128 * part + 128], f32(0.0),
+            )
+            for part in range(2)
+        ]
+        once = kept[0] + kept[1]
+        once = once + pltpu.roll(once, 64, 1)
+        turned = pltpu.roll(once, 32, 1)
+        o = [once[64 * i : 64 * i + 64] for i in range(4)]
+        t = [turned[64 * i : 64 * i + 64] for i in range(4)]
+        rows = pl.ds(pl.multiple_of(64 * a, 64), 64)
+
+        def merge(p0, p1, p2, p3):
+            return jnp.where(
+                lane_block < 2, jnp.where(lane_block == 0, p0, p1), jnp.where(lane_block == 2, p2, p3)
+            )
+
+        zed[0, rows, :] = merge(o[0], t[1], o[2], t[3])
+        zed[1, rows, :] = merge(t[0], o[1], t[2], o[3])
+
+    y_copy = pltpu.make_async_remote_copy(
+        src_ref=zed.at[1 - half], dst_ref=y_recv, send_sem=y_ss, recv_sem=y_rs,
+        device_id=(g, z * 2 + (1 - half)), device_id_type=MESH,
+    )
+    y_copy.start()
+
+    @pl.loop(1, 16)
+    def _(r):
+        a_copy(r).wait_recv()
+
+    for m in range(4):
+        piece = [a2a_recv[m, pl.ds(k, 64, stride=4), :] for k in range(4)]
+        for p in range(2):
+            even, odd = swap_pair(piece[2 * p], piece[2 * p + 1])
+            lhs[128 * m : 128 * m + 64, 128 * p : 128 * p + 128] = even
+            lhs[128 * m + 64 : 128 * m + 128, 128 * p : 128 * p + 128] = odd
+
+    @pl.loop(0, 2)
+    def _(h):
+        rows = pl.ds(pl.multiple_of(256 * h, 256), 256)
+        r_id = iota((256, 128), 0)
+        ia_label = occ_label(r_id % 64) ^ vir_label(8 * s + 4 * h + r_id // 64)
+        folds = []
+        for j in range(2):
+            product = jnp.dot(
+                lhs[rows, :], cyc_fold[:, 256 * j : 256 * j + 256], precision=EXACT, preferred_element_type=f32
+            )
+            kept = [
+                jnp.where(
+                    ia_label == (occ_label(jnp.int32(j)) ^ vir_label(lane + 128 * part)),
+                    product[:, 128 * part : 128 * part + 128], f32(0.0),
+                )
+                for part in range(2)
+            ]
+            folds.append(kept[0] + kept[1])
+        c_part[rows, :] = pack_pair(folds[0], folds[1])
+
+    regroup(c_part, c_send, 8)
+
+    def c_copy(r):
+        to = (g + r) % 16
+        return pltpu.make_async_remote_copy(
+            src_ref=c_send.at[to, 0], dst_ref=c_recv.at[g],
+            send_sem=c_ss.at[r], recv_sem=c_rs.at[r], device_id=(to, s), device_id_type=MESH,
+        )
+
+    @pl.loop(1, 16)
+    def _(r):
+        c_copy(r).start()
+
+    c_recv[g] = c_send[g, 0]
+
+    y_copy.wait_recv()
+    z_send[...] = zed[half] + y_recv[...]
+
+    def z_copy(r):
+        to = (z + r) % 16
+        return pltpu.make_async_remote_copy(
+            src_ref=z_send.at[pl.ds(pl.multiple_of(16 * to, 16), 16)], dst_ref=z_recv.at[z],
+            send_sem=z_ss.at[r], recv_sem=z_rs.at[r], device_id=(g, to * 2 + half), device_id_type=MESH,
+        )
+
+    @pl.loop(1, 16)
+    def _(r):
+        z_copy(r).start()
+
+    z_recv[z] = z_send[pl.ds(pl.multiple_of(16 * z, 16), 16), :]
+
+    @pl.loop(1, 16)
+    def _(r):
+        c_copy(r).wait_recv()
+
+    total = c_recv[0]
+    for n in range(1, 16):
+        total = total + c_recv[n]
+    turned = pltpu.roll(total, 64, 1)
+    both = [jnp.where(low64, total, turned), jnp.where(low64, turned, total)]
+    r_id = iota((32, 128), 0)
+    ia_label = occ_label(4 * g + r_id % 4) ^ vir_label(8 * s + r_id // 4)
+    for part in range(4):
+        j, b0 = part // 2, 128 * (part % 2)
+        c_full[part] = jnp.where(
+            ia_label == (occ_label(jnp.int32(j)) ^ vir_label(lane + b0)), both[j], f32(0.0)
+        )
+    for i in range(4):
+        for part in range(4):
+            cols = slice(128 * part, 128 * part + 128)
+            cyc_out[i, :, cols] = c_full[part, pl.ds(i, 8, stride=4), :]
+
+    @pl.loop(1, 16)
+    def _(r):
+        z_copy(r).wait_recv()
+
+    total = z_recv[0]
+    for n in range(1, 16):
+        total = total + z_recv[n]
+    mine = pl.ds(pl.multiple_of(16 * (z % 4), 16), 16)
+    quad[mine, :] = total
+
+    def q_copy(d):
+        to = 4 * (z // 4) + (z + d) % 4
+        return pltpu.make_async_remote_copy(
+            src_ref=quad.at[mine], dst_ref=quad.at[mine],
+            send_sem=q_ss.at[d], recv_sem=q_rs.at[d], device_id=(g, to * 2 + half), device_id_type=MESH,
+        )
+
+    for d in range(1, 4):
+        q_copy(d).start()
+    for d in range(1, 4):
+        q_copy(d).wait_recv()
+
+    col = vir_label(z // 4) ^ vir_label(32 * (s % 8) + lane)
+    full = quad[...]
+    for i in range(4):
+        here = full if i == 0 else pltpu.roll(full, 128 - 32 * i, 1)
+        kept = jnp.where(pair_label(i) == col, here, f32(0.0))
+        lad_out[64 * i : 64 * i + 64, :] = kept[:, 0:32]
+
+    for move in moves:
+        move.wait_send()
+    y_copy.wait_send()
+    for d in range(1, 4):
+        q_copy(d).wait_send()
+
+    @pl.loop(1, 16)
+    def _(r):
+        a_copy(r).wait_send()
+        c_copy(r).wait_send()
+        z_copy(r).wait_send()
+
+
+def folded_path(starts, amplitudes, ladder_ints, cycle_ints):
+    f32 = jnp.float32
+    vmem = pltpu.VMEM
+    dma = pltpu.SemaphoreType.DMA
+    return pl.pallas_call(
+        folded_kernel,
+        out_shape=(
+            jax.ShapeDtypeStruct((256, 32), f32),
+            jax.ShapeDtypeStruct((4, 8, 512), f32),
+        ),
+        in_specs=[pl.BlockSpec(memory_space=pltpu.SMEM)] + [pl.BlockSpec(memory_space=pl.ANY)] * 3,
+        out_specs=[pl.BlockSpec(memory_space=pltpu.VMEM)] * 2,
+        scratch_shapes=[
+            vmem((256, 2048), f32), vmem((2048, 64), f32), vmem((1024, 512), f32),
+            vmem((256, 512), f32), vmem((16, 4, 16, 128), f32), vmem((4, 256, 128), f32), vmem((256, 512), f32),
+            vmem((16, 256, 128), f32), vmem((512, 256), f32), vmem((2, 256, 128), f32), vmem((256, 128), f32),
+            vmem((256, 128), f32), vmem((16, 16, 128), f32), vmem((64, 128), f32),
+            vmem((512, 256), f32), vmem((512, 128), f32), vmem((16, 1, 32, 128), f32), vmem((16, 32, 128), f32),
+            vmem((4, 32, 128), f32),
+            dma((3,)), dma((17,)), dma((17,)), dma((16,)), dma((16,)), dma, dma,
+            dma((16,)), dma((16,)), dma((4,)), dma((4,)), dma((16,)), dma((16,)),
+        ],
+        compiler_params=pltpu.CompilerParams(
+            collective_id=0, has_side_effects=True, vmem_limit_bytes=40 * 1024 * 1024
+        ),
+        cost_estimate=pl.CostEstimate(flops=400_000_000, bytes_accessed=5_000_000, transcendentals=0),
+    )(starts, amplitudes, ladder_ints, cycle_ints)
+
+
+def per_device(amplitudes, ladder_ints, cycle_ints, occ_irrep, vir_irrep):
+    irreps = jnp.arange(IRREPS, dtype=jnp.int32)[:, None]
+    occ_starts = jnp.sum((occ_irrep[None, :] < irreps).astype(jnp.int32), axis=1)
+    vir_starts = jnp.sum((vir_irrep[None, :] < irreps).astype(jnp.int32), axis=1)
+    runs = jnp.sum((vir_irrep[None, :] == irreps).astype(jnp.int32), axis=1)
+    starts = jnp.concatenate([occ_starts, vir_starts])
+    return lax.cond(
+        jnp.max(runs) <= FOLD,
+        lambda: tuple(folded_path(starts, amplitudes, ladder_ints, cycle_ints)),
+        lambda: dense_path(amplitudes, ladder_ints, cycle_ints, occ_irrep, vir_irrep),
+    )
+
+
 def solution(mesh):
     return jax.shard_map(
         per_device,

time: 831 us -> 78.7 us (0.09)
  the two profiles are of different devices: /device:TPU:6 before, /device:TPU:1 now
where the time goes in v1:
time: 78.7 us; the launch traced here: 78.5 us
  Pallas kernels  59.4 us (75%)
  between operations  14.7 us (19%)
  other arithmetic  2.32 us (3%)
  local copies, waits for them, and re-layouts  2.09 us (3%)
    pallas_call x1, Pallas kernels, folded_path(): pl.pallas_call(folded_kernel, out_shape=(jax.ShapeDtypeStruct((256, 32),...  59.4 us

profile of v1, /device:TPU:1, one launch (start us, length us, event | category | flops | bytes accessed | tf_op | source)
XLA Modules:
  0.0 78.5 jit_solution(2471010248019421059)
XLA Ops:
  7.2 0.8 %convert_reduce_fusion = (s32[8]{0:T(128)S(1)}, s32[8]{0:T(128)S(1)}) fusion(s32[256]{0:T(256)} %param.11), kind=kLoop, calls=%fused_computation.11 | loop fusion | flops 12272 | bytes 1088 | tf_op jit(solution)/shard_map/reduce_sum | solution.py:440
  8.0 0.6 reduce_max.9
  9.3 0.8 convert_reduce_fusion.2
  10.1 0.1 pad_add_fusion
  10.1 60.8 %conditional.1 = (f32[256,32]{0,1:T(8,128)S(1)}, f32[4,8,512]{2,1,0:T(8,128)S(1)}) conditional(s32[]{:T(128)} %convert_element_type.13, (s32[64]{0:T(128)}, s32[256]{0:T(256)}, f32[2048,64]{0,1:T(8,128)}, f32[256,2048]{1,0:T(8,128)}, f32[1024,512]{1,0:T(8,128)}) %tuple.14, (s32[16]{0:T(128)S(1)}, f32[256,2048]{1,0:T(8,128)}, f32[2048,64]{0,1:T(8,128)}, ...), branch_computations={%region_4.7_spmd, %region_7.8_spmd} | conditional | flops 9663731712 | bytes 83956120 | solution.py:443
  10.1 1.4 %copy.31.lad_hbm = f32[2048,64]{1,0:T(8,128)S(1)} copy(f32[2048,64]{0,1:T(8,128)} %get-tuple-element.71) | data formatting | bytes 1048576 | tf_op jit(solution)/shard_map
  11.5 59.4 %branch_1_fun.1 = (f32[256,32]{1,0:T(8,128)S(1)}, f32[4,8,512]{2,1,0:T(8,128)S(1)}) custom-call(s32[16]{0:T(128)S(1)} %get-tuple-element.23.starts, f32[256,2048]{1,0:T(8,128)} %get-tuple-element.24.amp_hbm, f32[2048,64]{1,0:T(8,128)S(1)} %copy.31.lad_hbm, f32[1024,512]{1,0:T(8,128)} %get-tuple-element.26.cyc_hbm), custom_call_target="tpu_custom_call" | custom-call | flops 400000000 | bytes 5000000 | tf_op jit(solution)/shard_map/cond/branch_1_fun/pallas_call | solution.py:412
  70.9 0.1 copy.30
  71.0 0.0 copy-start.2
  71.0 0.7 copy.44
  71.6 0.0 copy-done.2
Async XLA Ops:
  71.0 0.7 copy-start.2

commit v2 on v0

--- a/solution.py
+++ b/solution.py
@@ -1,7 +1,15 @@
+import functools
+
 import jax
 import jax.numpy as jnp
 from jax import lax
+from jax.experimental import pallas as pl
+from jax.experimental.pallas import tpu as pltpu
 from jax.sharding import PartitionSpec as P
+
+FOLD = 64
+IRREPS = 8
+MESH = pl.DeviceIdType.MESH
 
 
 def allowed_mask(lab_i, lab_j, lab_a, lab_b):
@@ -10,7 +18,22 @@
     return left == right
 
 
-def per_device(amplitudes, ladder_ints, cycle_ints, occ_irrep, vir_irrep):
+def gather_cols(block):
+    groups = lax.axis_size("grp")
+    copies = jnp.broadcast_to(block[None], (groups,) + block.shape)
+    parts = lax.all_to_all(copies, "grp", split_axis=0, concat_axis=0, tiled=True)
+    return jnp.moveaxis(parts, 0, 1).reshape(block.shape[0], groups * block.shape[1])
+
+
+def sum_parts(partial, axis, dim):
+    count = lax.axis_size(axis)
+    shape = partial.shape
+    split = partial.reshape(shape[:dim] + (count, shape[dim] // count) + shape[dim + 1 :])
+    parts = lax.all_to_all(split, axis, split_axis=dim, concat_axis=dim, tiled=True)
+    return jnp.sum(parts, axis=dim)
+
+
+def dense_path(amplitudes, ladder_ints, cycle_ints, occ_irrep, vir_irrep):
     groups = lax.axis_size("grp")
     slabs = lax.axis_size("slab")
     grp_index = lax.axis_index("grp")
@@ -24,11 +47,11 @@
     a_count = window // vir_count
     partial_sum = jnp.dot(
         amplitudes,
-        lax.all_gather(ladder_ints, "grp", axis=1, tiled=True),
+        gather_cols(ladder_ints),
         precision=lax.Precision.HIGHEST,
         preferred_element_type=jnp.float32,
     )
-    ladder = lax.psum_scatter(partial_sum, "slab", scatter_dimension=1, tiled=True)
+    ladder = sum_parts(partial_sum, "slab", 1)
     occ_mine = lax.dynamic_slice_in_dim(occ_irrep, grp_index * occ_local, occ_local, 0)
     row_i = jnp.repeat(occ_mine, occ_count)
     row_j = jnp.tile(occ_irrep, occ_local)
@@ -48,7 +71,7 @@
     partial_cycle = jnp.einsum(
         "ikac,kcw->iaw", regrouped, cycle_table, precision=lax.Precision.HIGHEST
     )
-    cycle = lax.psum_scatter(partial_cycle, "grp", scatter_dimension=0, tiled=True)
+    cycle = sum_parts(partial_cycle, "grp", 0)
     j_count = cycle_cols // vir_count
     vir_mine = lax.dynamic_slice_in_dim(vir_irrep, slab_index * vir_local, vir_local, 0)
     col_j = jnp.repeat(occ_irrep[:j_count], vir_count)
@@ -63,6 +86,415 @@
     return (ladder_term, cycle_term)
 
 
+def folded_kernel(
+    occ_hbm, vir_hbm, amp_hbm, lad_hbm, cyc_hbm, lad_out, cyc_out,
+    occ_v, vir_v, amp, lad, cyc, amp_fold, amp_hi, amp_lo, a2a_send, a2a_recv, cyc_hi, cyc_lo, gath,
+    zed, y_recv, z_send, z_recv, quad, lhs_hi, lhs_lo, c_part, c_send, c_recv, c_full,
+    load_sem, g_ss, g_rs, a_ss, a_rs, y_ss, y_rs, z_ss, z_rs, q_ss, q_rs, c_ss, c_rs,
+):
+    f32, i32, bf16 = jnp.float32, jnp.int32, jnp.bfloat16
+    g, s = lax.axis_index("grp"), lax.axis_index("slab")
+    core, x, y = g % 2, (g // 2) % 4, g // 8
+    z, half = s // 2, s % 2
+
+    load_l = pltpu.make_async_copy(lad_hbm, lad, load_sem.at[0])
+    load_a = pltpu.make_async_copy(amp_hbm, amp, load_sem.at[1])
+    load_w = pltpu.make_async_copy(cyc_hbm, cyc, load_sem.at[2])
+    load_o = pltpu.make_async_copy(occ_hbm, occ_v, load_sem.at[3])
+    load_v = pltpu.make_async_copy(vir_hbm, vir_v, load_sem.at[4])
+    load_l.start()
+    load_o.start()
+    load_v.start()
+    load_a.start()
+    load_w.start()
+
+    barrier = pltpu.get_barrier_semaphore()
+
+    @pl.loop(1, 16)
+    def _(r):
+        pl.semaphore_signal(barrier, inc=1, device_id=((g + r) % 16, s), device_id_type=MESH)
+        pl.semaphore_signal(barrier, inc=1, device_id=(g, ((z + r) % 16) * 2 + half), device_id_type=MESH)
+
+    pl.semaphore_signal(barrier, inc=1, device_id=(g, z * 2 + (1 - half)), device_id_type=MESH)
+
+    def iota(shape, dim):
+        return lax.broadcasted_iota(i32, shape, dim)
+
+    def split(value):
+        high = value.astype(bf16)
+        return high, (value - high.astype(f32)).astype(bf16)
+
+    low64 = iota((1, 128), 1) < 64
+    lane = iota((1, 128), 1)
+
+    def pack_pair(first, second):
+        keep = jnp.where(low64, first, second)
+        move = jnp.where(low64, second, first)
+        return keep + pltpu.roll(move, 64, 1)
+
+    def swap_pair(first, second):
+        return (
+            jnp.where(low64, first, pltpu.roll(second, 64, 1)),
+            jnp.where(low64, pltpu.roll(first, 64, 1), second),
+        )
+
+    def fold_pair(src, rows, m):
+        at = [src[rows, 512 * m + 128 * n : 512 * m + 128 * n + 128] for n in range(4)]
+        return pack_pair(at[0] + at[1], at[2] + at[3])
+
+    def regroup(src, dst, blocks):
+        low4 = iota((8, 1), 0) < 4
+
+        @pl.loop(0, 8)
+        def _(q):
+            for n in range(0, blocks, 2):
+                for c in range(src.shape[1] // 128):
+                    cols = slice(128 * c, 128 * c + 128)
+                    one = src[pl.ds(pl.multiple_of(64 * n + 8 * q, 8), 8), cols]
+                    two = src[pl.ds(pl.multiple_of(64 * n + 64 + 8 * q, 8), 8), cols]
+                    dst[2 * q, c, 4 * n : 4 * n + 8, :] = jnp.where(low4, one, pltpu.roll(two, 4, 0))
+                    dst[2 * q + 1, c, 4 * n : 4 * n + 8, :] = jnp.where(low4, pltpu.roll(one, 4, 0), two)
+
+    load_l.wait()
+    for m in range(4):
+        gath[g, :, 128 * m : 128 * m + 128] = fold_pair(lad, slice(0, 64), m)
+
+    pl.semaphore_wait(barrier, 31)
+
+    def dev(y_, x_, core_):
+        return (y_ * 4 + x_ % 4) * 2 + core_
+
+    turn = 1 - 2 * (x % 2)
+    sib, y_dev = dev(y, x, 1 - core), dev(1 - y, x, core)
+    mate, other = dev(y, x + 4 + turn, core), dev(y, x + 4 - turn, core)
+    y_mate, y_other = dev(1 - y, x + 4 + turn, core), dev(1 - y, x + 4 - turn, core)
+    across, y_across = dev(y, x + 2, core), dev(1 - y, x + 2, core)
+
+    def g_copy(k, slot, to, rows=None):
+        ref = gath.at[slot] if rows is None else gath.at[slot, rows]
+        return pltpu.make_async_remote_copy(
+            src_ref=ref, dst_ref=ref, send_sem=g_ss.at[k], recv_sem=g_rs.at[k],
+            device_id=(to, s), device_id_type=MESH,
+        )
+
+    lower, upper = pl.ds(0, 32), pl.ds(32, 32)
+    moves = [
+        g_copy(0, g, y_dev), g_copy(1, g, mate), g_copy(2, g, other), g_copy(3, g, sib),
+        g_copy(4, y_dev, mate), g_copy(5, y_dev, other), g_copy(6, y_dev, sib),
+        g_copy(7, mate, other, lower), g_copy(8, other, mate, upper),
+        g_copy(9, y_mate, other, lower), g_copy(10, y_other, mate, upper),
+        g_copy(11, mate, sib), g_copy(12, other, sib), g_copy(13, y_mate, sib), g_copy(14, y_other, sib),
+        g_copy(15, across, sib), g_copy(16, y_across, sib),
+    ]
+
+    def go(*numbers):
+        for k in numbers:
+            moves[k].start()
+
+    def got(*numbers):
+        for k in numbers:
+            moves[k].wait_recv()
+
+    go(0, 1, 2, 3)
+
+    load_a.wait()
+
+    @pl.loop(0, 16)
+    def _(r):
+        rows = pl.ds(pl.multiple_of(16 * r, 16), 16)
+        for m in range(4):
+            cols = slice(128 * m, 128 * m + 128)
+            folded = fold_pair(amp, rows, m)
+            amp_fold[rows, cols] = folded
+            amp_hi[rows, cols], amp_lo[rows, cols] = split(folded)
+
+    regroup(amp_fold, a2a_send, 4)
+    got(0)
+    go(4, 5, 6)
+    got(1)
+    go(7, 11)
+    got(2)
+    go(8, 12)
+
+    mine16 = pl.ds(pl.multiple_of(16 * g, 16), 16)
+
+    def a_copy(r):
+        to = (g + r) % 16
+        return pltpu.make_async_remote_copy(
+            src_ref=a2a_send.at[to], dst_ref=a2a_recv.at[:, mine16],
+            send_sem=a_ss.at[r], recv_sem=a_rs.at[r], device_id=(to, s), device_id_type=MESH,
+        )
+
+    @pl.loop(1, 16)
+    def _(r):
+        a_copy(r).start()
+
+    a2a_recv[:, mine16, :] = a2a_send[g]
+
+    load_o.wait()
+    load_v.wait()
+
+    def run_starts(ref):
+        return [
+            jnp.sum(jnp.where(ref[...] < v, 1.0, 0.0), axis=1, keepdims=True).astype(i32) for v in range(1, IRREPS)
+        ]
+
+    occ_starts, vir_starts = run_starts(occ_v), run_starts(vir_v)
+
+    def label(index, starts):
+        total = jnp.where(index >= starts[0], 1, 0)
+        for start in starts[1:]:
+            total = total + jnp.where(index >= start, 1, 0)
+        return total
+
+    def occ_label(index):
+        return label(index, occ_starts)
+
+    def vir_label(index):
+        return label(index, vir_starts)
+
+    zero = jnp.zeros((1, 128), i32)
+
+    def pair_label(part):
+        return occ_label(4 * g + 2 * part + lane // 64) ^ occ_label(lane % 64)
+
+    ij_label = [pair_label(part) for part in range(2)]
+    row_label = [vir_label(iota((64, 128), 0) + 64 * m) for m in range(4)]
+
+    def dot(first, second, dims):
+        return lax.dot_general(first, second, (dims, ((), ())), preferred_element_type=f32)
+
+    def dot3(a_hi, a_lo, b_hi, b_lo, dims):
+        return dot(a_hi, b_hi, dims) + (dot(a_hi, b_lo, dims) + dot(a_lo, b_hi, dims))
+
+    order = [2 * y + x // 2, 2 * (1 - y) + x // 2, 2 * y + 1 - x // 2, 2 * (1 - y) + 1 - x // 2]
+
+    def y_copy(n):
+        return pltpu.make_async_remote_copy(
+            src_ref=zed.at[1 - half, order[n]], dst_ref=y_recv.at[order[n]],
+            send_sem=y_ss.at[n], recv_sem=y_rs.at[n],
+            device_id=(g, z * 2 + (1 - half)), device_id_type=MESH,
+        )
+
+    def z_copy(to):
+        r = (to - z + 16) % 16
+        return pltpu.make_async_remote_copy(
+            src_ref=z_send.at[to], dst_ref=z_recv.at[z],
+            send_sem=z_ss.at[r], recv_sem=z_rs.at[r], device_id=(g, to * 2 + half), device_id_type=MESH,
+        )
+
+    def ladder_product(n):
+        a = order[n]
+        hi, lo = split(gath[pl.ds(4 * a, 4)].reshape(256, 512))
+        product = dot3(hi, lo, amp_hi[...], amp_lo[...], ((1,), (1,)))
+        a_label = vir_label(zero + a)
+        for part in range(2):
+            cols = slice(128 * part, 128 * part + 128)
+            want = ij_label[part] ^ a_label
+            total = jnp.where(row_label[0] == want, product[0:64, cols], f32(0.0))
+            for m in range(1, 4):
+                total = total + jnp.where(row_label[m] == want, product[64 * m : 64 * m + 64, cols], f32(0.0))
+            zed[0, a, :, cols] = total[0:32]
+            zed[1, a, :, cols] = total[32:64]
+        y_copy(n).start()
+
+    def ladder_sums(n):
+        a = order[n]
+        y_copy(n).wait_recv()
+        total = zed[half, a] + y_recv[a]
+        for q in range(4):
+            z_send[4 * a + q] = total[8 * q : 8 * q + 8]
+            to = 4 * a + q
+
+            @pl.when(to != z)
+            def _():
+                z_copy(to).start()
+
+    got(3, 11)
+    ladder_product(0)
+    got(4)
+    go(9, 13)
+    got(5)
+    go(10, 14)
+
+    load_w.wait()
+
+    @pl.loop(0, 4)
+    def _(k):
+        part = cyc[pl.ds(pl.multiple_of(256 * k, 64), 64), :]
+        for m in range(1, 4):
+            part = part + cyc[pl.ds(pl.multiple_of(256 * k + 64 * m, 64), 64), :]
+        rows = pl.ds(pl.multiple_of(64 * k, 64), 64)
+        cyc_hi[rows, :], cyc_lo[rows, :] = split(part)
+
+    got(7, 8)
+    go(15)
+    got(6, 13)
+    ladder_product(1)
+    ladder_sums(0)
+    got(9, 10)
+    go(16)
+    got(12, 15)
+    ladder_product(2)
+    ladder_sums(1)
+    got(14, 16)
+    ladder_product(3)
+    ladder_sums(2)
+
+    @pl.loop(1, 16)
+    def _(r):
+        a_copy(r).wait_recv()
+
+    for m in range(4):
+        piece = [a2a_recv[m, pl.ds(k, 64, stride=4), :] for k in range(4)]
+        for p in range(2):
+            even, odd = swap_pair(piece[2 * p], piece[2 * p + 1])
+            cols = slice(128 * p, 128 * p + 128)
+            for at, value in ((128 * m, even), (128 * m + 64, odd)):
+                lhs_hi[at : at + 64, cols], lhs_lo[at : at + 64, cols] = split(value)
+
+    ladder_sums(3)
+    z_recv[z] = z_send[z]
+
+    jb_label = [
+        occ_label(zero + part // 2) ^ vir_label(lane + 128 * (part % 2)) for part in range(4)
+    ]
+
+    @pl.loop(0, 2)
+    def _(h):
+        rows = pl.ds(pl.multiple_of(256 * h, 256), 256)
+        r_id = iota((256, 128), 0)
+        ia_label = occ_label(r_id % 64) ^ vir_label(8 * s + 4 * h + r_id // 64)
+        folds = []
+        for j in range(2):
+            cols = slice(256 * j, 256 * j + 256)
+            product = dot3(lhs_hi[rows, :], lhs_lo[rows, :], cyc_hi[:, cols], cyc_lo[:, cols], ((1,), (0,)))
+            kept = [
+                jnp.where(ia_label == jb_label[2 * j + part], product[:, 128 * part : 128 * part + 128], f32(0.0))
+                for part in range(2)
+            ]
+            folds.append(kept[0] + kept[1])
+        c_part[rows, :] = pack_pair(folds[0], folds[1])
+
+    regroup(c_part, c_send, 8)
+
+    def c_copy(r):
+        to = (g + r) % 16
+        return pltpu.make_async_remote_copy(
+            src_ref=c_send.at[to, 0], dst_ref=c_recv.at[g],
+            send_sem=c_ss.at[r], recv_sem=c_rs.at[r], device_id=(to, s), device_id_type=MESH,
+        )
+
+    @pl.loop(1, 16)
+    def _(r):
+        c_copy(r).start()
+
+    c_recv[g] = c_send[g, 0]
+
+    def z_arrival(r):
+        return pltpu.make_async_remote_copy(
+            src_ref=z_send.at[z], dst_ref=z_recv.at[z], send_sem=z_ss.at[r], recv_sem=z_rs.at[r],
+            device_id=(g, ((z + r) % 16) * 2 + half), device_id_type=MESH,
+        )
+
+    @pl.loop(1, 16)
+    def _(r):
+        z_arrival(r).wait_recv()
+
+    total = z_recv[0]
+    for n in range(1, 16):
+        total = total + z_recv[n]
+    quarter = z % 4
+    quad[quarter] = total
+
+    def q_copy(d):
+        to = 4 * (z // 4) + (z + d) % 4
+        return pltpu.make_async_remote_copy(
+            src_ref=quad.at[quarter], dst_ref=quad.at[quarter],
+            send_sem=q_ss.at[d], recv_sem=q_rs.at[d], device_id=(g, to * 2 + half), device_id_type=MESH,
+        )
+
+    for d in range(1, 4):
+        q_copy(d).start()
+
+    @pl.loop(1, 16)
+    def _(r):
+        c_copy(r).wait_recv()
+
+    total = c_recv[0]
+    for n in range(1, 16):
+        total = total + c_recv[n]
+    turned = pltpu.roll(total, 64, 1)
+    both = [jnp.where(low64, total, turned), jnp.where(low64, turned, total)]
+    r_id = iota((32, 128), 0)
+    ia_label = occ_label(4 * g + r_id % 4) ^ vir_label(8 * s + r_id // 4)
+    for part in range(4):
+        c_full[part] = jnp.where(ia_label == jb_label[part], both[part // 2], f32(0.0))
+    for i in range(4):
+        for part in range(4):
+            cyc_out[i, :, 128 * part : 128 * part + 128] = c_full[part, pl.ds(i, 8, stride=4), :]
+
+    for d in range(1, 4):
+        q_copy(d).wait_recv()
+
+    b_label = vir_label(zero + z // 4) ^ vir_label(32 * (s % 8) + iota((32, 128), 0))
+    full = quad[...].reshape(32, 256)
+    for part in range(2):
+        cols = slice(128 * part, 128 * part + 128)
+        lad_out[:, cols] = jnp.where(ij_label[part] == b_label, full[:, cols], f32(0.0))
+
+    for move in moves:
+        move.wait_send()
+    for d in range(1, 4):
+        q_copy(d).wait_send()
+
+    for n in range(4):
+        y_copy(n).wait_send()
+
+    @pl.loop(1, 16)
+    def _(r):
+        a_copy(r).wait_send()
+        c_copy(r).wait_send()
+        z_arrival(r).wait_send()
+
+
+def folded_path(amplitudes, ladder_ints, cycle_ints, occ_irrep, vir_irrep):
+    f32, bf16 = jnp.float32, jnp.bfloat16
+    vmem = pltpu.VMEM
+    dma = pltpu.SemaphoreType.DMA
+    ladder, cycle = pl.pallas_call(
+        folded_kernel,
+        out_shape=(
+            jax.ShapeDtypeStruct((32, 256), f32),
+            jax.ShapeDtypeStruct((4, 8, 512), f32),
+        ),
+        in_specs=[pl.BlockSpec(memory_space=pl.ANY)] * 5,
+        out_specs=[pl.BlockSpec(memory_space=pltpu.VMEM)] * 2,
+        scratch_shapes=[
+            vmem((1, 64), jnp.int32), vmem((1, 256), jnp.int32),
+            vmem((256, 2048), f32), vmem((64, 2048), f32), vmem((1024, 512), f32),
+            vmem((256, 512), f32), vmem((256, 512), bf16), vmem((256, 512), bf16),
+            vmem((16, 4, 16, 128), f32), vmem((4, 256, 128), f32),
+            vmem((256, 512), bf16), vmem((256, 512), bf16), vmem((16, 64, 512), f32),
+            vmem((2, 4, 32, 256), f32), vmem((4, 32, 256), f32), vmem((16, 8, 256), f32), vmem((16, 8, 256), f32),
+            vmem((4, 8, 256), f32), vmem((512, 256), bf16), vmem((512, 256), bf16),
+            vmem((512, 128), f32), vmem((16, 1, 32, 128), f32), vmem((16, 32, 128), f32), vmem((4, 32, 128), f32),
+            dma((5,)), dma((17,)), dma((17,)), dma((16,)), dma((16,)), dma((4,)), dma((4,)),
+            dma((16,)), dma((16,)), dma((4,)), dma((4,)), dma((16,)), dma((16,)),
+        ],
+        compiler_params=pltpu.CompilerParams(
+            collective_id=0, has_side_effects=True, vmem_limit_bytes=40 * 1024 * 1024
+        ),
+        cost_estimate=pl.CostEstimate(flops=400_000_000, bytes_accessed=5_000_000, transcendentals=0),
+    )(occ_irrep.reshape(1, -1), vir_irrep.reshape(1, -1), amplitudes, ladder_ints.T, cycle_ints)
+    return ladder.T, cycle
+
+
+def per_device(amplitudes, ladder_ints, cycle_ints, occ_irrep, vir_irrep):
+    fits = jnp.all(vir_irrep[FOLD:] != vir_irrep[:-FOLD])
+    return lax.cond(fits, folded_path, dense_path, amplitudes, ladder_ints, cycle_ints, occ_irrep, vir_irrep)
+
+
 def solution(mesh):
     return jax.shard_map(
         per_device,

time: 831 us -> 53.2 us (0.06)
  waiting for transfers between devices: 751 us -> 0 us
  Pallas kernels: 0 us -> 48.1 us
  blocking collectives: 44.1 us -> 0 us
  matrix products: 15.1 us -> 0 us
  between operations: 13.8 us -> 1.29 us
    reduce_scatter x2 -> x0, waiting for transfers between devices: 725 us -> none  [the longest x1 667 us: per_device(): lax.psum_scatter(partial_sum, 'slab', scatter_dimension=1, tiled=True)]
    pallas_call x0 -> x1, Pallas kernels: none -> 48.1 us  [folded_path(): pl.pallas_call(folded_kernel, out_shape=(jax.ShapeDtypeStruct((32, 256),...]
    all_to_all x1 -> x0, blocking collectives: 44.1 us -> none  [per_device(): lax.all_to_all(blocks, 'grp', split_axis=1, concat_axis=0, tiled=True)]
    all_gather x1 -> x0, waiting for transfers between devices: 25.5 us -> none  [per_device(): lax.all_gather(ladder_ints, 'grp', axis=1, tiled=True)]
    dot_general x2 -> x0, matrix products: 15.1 us -> none  [the longest x1 10.6 us: per_device(): jnp.dot(amplitudes, lax.all_gather(ladder_ints, 'grp', axis=1, tiled=True...]
  transfers between devices with their start and end apart: 3 -> 0, of which waited for: 3 -> 0; matrix products, arithmetic and copies ran while one was open for 2% -> 0% of each run, Pallas kernels for 0% -> 0%
where the time goes in v2:
time: 53.2 us; the launch traced here: 52.3 us
  Pallas kernels  48.1 us (90%)
  other arithmetic  1.46 us (3%)
  between operations  1.29 us (2%)
  local copies, waits for them, and re-layouts  1.25 us (2%)
    pallas_call x1, Pallas kernels, folded_path(): pl.pallas_call(folded_kernel, out_shape=(jax.ShapeDtypeStruct((32, 256),...  48.1 us
    reduce_and x1, other arithmetic, per_device(): fits = jnp.all(vir_irrep[FOLD:] != vir_irrep[:-FOLD])  1.46 us
    unnamed x2, local copies, waits for them, and re-layouts  1.25 us

profile of v2, /device:TPU:6, one launch (start us, length us, event | category | flops | bytes accessed | tf_op | source)
XLA Modules:
  0.0 52.3 jit_solution(1731064658352094814)
XLA Ops:
  0.6 1.5 %compare_reduce_fusion = pred[]{:T(512)} fusion(s32[256]{0:T(256)} %param.11), kind=kLoop, calls=%fused_computation.16 | loop fusion | flops 383 | bytes 1537 | tf_op jit(solution)/shard_map/reduce_and | solution.py:494
  2.7 48.3 %conditional.1 = (f32[256,32]{0,1:T(8,128)S(1)}, f32[4,8,512]{2,1,0:T(8,128)S(1)}) conditional(s32[]{:T(128)} %convert_element_type.3, (s32[64]{0:T(128)}, s32[256]{0:T(256)}, f32[2048,64]{0,1:T(8,128)}, f32[256,2048]{1,0:T(8,128)}, f32[1024,512]{1,0:T(8,128)}) %tuple.15, (s32[64]{0:T(128)}, s32[256]{0:T(256)}, f32[2048,64]{0,1:T(8,128)}, ...), branch_computations={%region_1.4_spmd, %region_4.5_spmd} | conditional | flops 9664231424 | bytes 82710920 | solution.py:495
  2.9 48.1 %branch_1_fun.1 = (f32[32,256]{1,0:T(8,128)S(1)}, f32[4,8,512]{2,1,0:T(8,128)S(1)}) custom-call(s32[1,64]{1,0:T(1,128)} %bitcast.64, s32[1,256]{1,0:T(1,128)} %bitcast.58, f32[256,2048]{1,0:T(8,128)} %get-tuple-element.27.amp_hbm, f32[64,2048]{1,0:T(8,128)} %bitcast.56, f32[1024,512]{1,0:T(8,128)} %get-tuple-element.29.cyc_hbm), custom_call_target="tpu_custom_call" | custom-call | flops 400000000 | bytes 5000000 | tf_op jit(solution)/shard_map/cond/branch_1_fun/pallas_call | solution.py:465
  51.1 0.6 %copy.36 = f32[256,32]{0,1:T(8,128)} copy(f32[256,32]{0,1:T(8,128)S(1)} %get-tuple-element.46) | data formatting | bytes 65536
  51.7 0.6 %copy.37 = f32[4,8,512]{2,1,0:T(8,128)} copy(f32[4,8,512]{2,1,0:T(8,128)S(1)} %get-tuple-element.47) | data formatting | bytes 131072

commit v3 on v2

--- a/solution.py
+++ b/solution.py
@@ -7,7 +7,7 @@
 from jax.experimental.pallas import tpu as pltpu
 from jax.sharding import PartitionSpec as P
 
-FOLD = 64
+TILES = 3
 IRREPS = 8
 MESH = pl.DeviceIdType.MESH
 
@@ -87,10 +87,11 @@
 
 
 def folded_kernel(
-    occ_hbm, vir_hbm, amp_hbm, lad_hbm, cyc_hbm, lad_out, cyc_out,
+    tiles,
+    occ_hbm, vir_hbm, amp_hbm, lad_hbm, cyc_hbm, lad_out, cyc_out, run_out,
     occ_v, vir_v, amp, lad, cyc, amp_fold, amp_hi, amp_lo, a2a_send, a2a_recv, cyc_hi, cyc_lo, gath,
     zed, y_recv, z_send, z_recv, quad, lhs_hi, lhs_lo, c_part, c_send, c_recv, c_full,
-    load_sem, g_ss, g_rs, a_ss, a_rs, y_ss, y_rs, z_ss, z_rs, q_ss, q_rs, c_ss, c_rs,
+    load_sem, g_ss, g_rs, a_ss, a_rs, y_ss, y_rs, z_ss, z_rs, q_ss, q_rs, c_ss, c_rs, here_sem, meet_sem,
 ):
     f32, i32, bf16 = jnp.float32, jnp.int32, jnp.bfloat16
     g, s = lax.axis_index("grp"), lax.axis_index("slab")
@@ -112,10 +113,11 @@
 
     @pl.loop(1, 16)
     def _(r):
-        pl.semaphore_signal(barrier, inc=1, device_id=((g + r) % 16, s), device_id_type=MESH)
-        pl.semaphore_signal(barrier, inc=1, device_id=(g, ((z + r) % 16) * 2 + half), device_id_type=MESH)
-
-    pl.semaphore_signal(barrier, inc=1, device_id=(g, z * 2 + (1 - half)), device_id_type=MESH)
+        to = (g + r) % 16
+
+        @pl.when(to != 0)
+        def _():
+            pl.semaphore_signal(barrier, inc=1, device_id=(to, s), device_id_type=MESH)
 
     def iota(shape, dim):
         return lax.broadcasted_iota(i32, shape, dim)
@@ -132,15 +134,21 @@
         move = jnp.where(low64, second, first)
         return keep + pltpu.roll(move, 64, 1)
 
-    def swap_pair(first, second):
-        return (
-            jnp.where(low64, first, pltpu.roll(second, 64, 1)),
-            jnp.where(low64, pltpu.roll(first, 64, 1), second),
-        )
-
-    def fold_pair(src, rows, m):
-        at = [src[rows, 512 * m + 128 * n : 512 * m + 128 * n + 128] for n in range(4)]
-        return pack_pair(at[0] + at[1], at[2] + at[3])
+    def spread(rows):
+        turned = [row if n == 0 else pltpu.roll(row, 16 * n, 1) for n, row in enumerate(rows)]
+        for bit in (1, 2, 4):
+            here = (lane // 16) // bit % 2 == 1
+            turned = [jnp.where(here, turned[(n + bit) % 8], turned[n]) for n in range(8)]
+        return [turned[0]] + [pltpu.roll(turned[8 - p], 128 - 16 * p, 1) for p in range(1, 8)]
+
+    def fold(src, rows):
+        sums = [None] * tiles
+        for part in range(2):
+            runs = spread([src[rows, 256 * n + 128 * part : 256 * n + 128 * part + 128] for n in range(8)])
+            for p in range(8):
+                u = (8 * part + p) % tiles
+                sums[u] = runs[p] if sums[u] is None else sums[u] + runs[p]
+        return sums
 
     def regroup(src, dst, blocks):
         low4 = iota((8, 1), 0) < 4
@@ -156,10 +164,41 @@
                     dst[2 * q + 1, c, 4 * n : 4 * n + 8, :] = jnp.where(low4, pltpu.roll(one, 4, 0), two)
 
     load_l.wait()
-    for m in range(4):
-        gath[g, :, 128 * m : 128 * m + 128] = fold_pair(lad, slice(0, 64), m)
-
-    pl.semaphore_wait(barrier, 31)
+
+    @pl.loop(0, 4)
+    def _(r):
+        rows = pl.ds(pl.multiple_of(16 * r, 16), 16)
+        for u, folded in enumerate(fold(lad, rows)):
+            gath[g, rows, 128 * u : 128 * u + 128] = folded
+
+    @pl.when(g != 0)
+    def _():
+        pl.semaphore_wait(barrier, 15)
+
+    @pl.when(g == 1)
+    def _():
+        pl.semaphore_signal(here_sem, inc=1, device_id=(0, s), device_id_type=MESH)
+
+    @pl.when(g == 0)
+    def _():
+        pl.semaphore_wait(here_sem, 1)
+
+        @pl.loop(1, 32)
+        def _(r):
+            pl.semaphore_signal(barrier, inc=1, device_id=(0, (s + r) % 32), device_id_type=MESH)
+
+    def meet_slabs():
+        @pl.when(g == 0)
+        def _():
+            pl.semaphore_wait(barrier, 31)
+
+            @pl.loop(1, 16)
+            def _(r):
+                pl.semaphore_signal(meet_sem, inc=1, device_id=(r, s), device_id_type=MESH)
+
+        @pl.when(g != 0)
+        def _():
+            pl.semaphore_wait(meet_sem, 1)
 
     def dev(y_, x_, core_):
         return (y_ * 4 + x_ % 4) * 2 + core_
@@ -202,9 +241,8 @@
     @pl.loop(0, 16)
     def _(r):
         rows = pl.ds(pl.multiple_of(16 * r, 16), 16)
-        for m in range(4):
-            cols = slice(128 * m, 128 * m + 128)
-            folded = fold_pair(amp, rows, m)
+        for u, folded in enumerate(fold(amp, rows)):
+            cols = slice(128 * u, 128 * u + 128)
             amp_fold[rows, cols] = folded
             amp_hi[rows, cols], amp_lo[rows, cols] = split(folded)
 
@@ -241,6 +279,12 @@
 
     occ_starts, vir_starts = run_starts(occ_v), run_starts(vir_v)
 
+    starts = [0] + vir_starts + [vir_v.shape[1]]
+    longest = starts[1]
+    for v in range(1, IRREPS):
+        longest = jnp.maximum(longest, starts[v + 1] - starts[v])
+    run_out[0, 0] = jnp.max(longest)
+
     def label(index, starts):
         total = jnp.where(index >= starts[0], 1, 0)
         for start in starts[1:]:
@@ -285,7 +329,7 @@
 
     def ladder_product(n):
         a = order[n]
-        hi, lo = split(gath[pl.ds(4 * a, 4)].reshape(256, 512))
+        hi, lo = split(gath[pl.ds(4 * a, 4)].reshape(256, 128 * tiles))
         product = dot3(hi, lo, amp_hi[...], amp_lo[...], ((1,), (1,)))
         a_label = vir_label(zero + a)
         for part in range(2):
@@ -311,6 +355,7 @@
                 z_copy(to).start()
 
     got(3, 11)
+    meet_slabs()
     ladder_product(0)
     got(4)
     go(9, 13)
@@ -321,40 +366,51 @@
 
     @pl.loop(0, 4)
     def _(k):
-        part = cyc[pl.ds(pl.multiple_of(256 * k, 64), 64), :]
-        for m in range(1, 4):
-            part = part + cyc[pl.ds(pl.multiple_of(256 * k + 64 * m, 64), 64), :]
-        rows = pl.ds(pl.multiple_of(64 * k, 64), 64)
-        cyc_hi[rows, :], cyc_lo[rows, :] = split(part)
+        for u in range(tiles):
+            part = cyc[pl.ds(pl.multiple_of(256 * k + 16 * u, 16), 16), :]
+            for e in range(u + tiles, 16, tiles):
+                part = part + cyc[pl.ds(pl.multiple_of(256 * k + 16 * e, 16), 16), :]
+            rows = pl.ds(pl.multiple_of(16 * (tiles * k + u), 16), 16)
+            cyc_hi[rows, :], cyc_lo[rows, :] = split(part)
+
+    if tiles < 4:
+        cyc_hi[64 * tiles : 256, :] = jnp.zeros((256 - 64 * tiles, 512), bf16)
+        cyc_lo[64 * tiles : 256, :] = jnp.zeros((256 - 64 * tiles, 512), bf16)
 
     got(7, 8)
     go(15)
     got(6, 13)
     ladder_product(1)
-    ladder_sums(0)
     got(9, 10)
     go(16)
+
+    ladder_sums(0)
     got(12, 15)
     ladder_product(2)
     ladder_sums(1)
     got(14, 16)
     ladder_product(3)
     ladder_sums(2)
-
-    @pl.loop(1, 16)
-    def _(r):
-        a_copy(r).wait_recv()
-
-    for m in range(4):
-        piece = [a2a_recv[m, pl.ds(k, 64, stride=4), :] for k in range(4)]
-        for p in range(2):
-            even, odd = swap_pair(piece[2 * p], piece[2 * p + 1])
-            cols = slice(128 * p, 128 * p + 128)
-            for at, value in ((128 * m, even), (128 * m + 64, odd)):
-                lhs_hi[at : at + 64, cols], lhs_lo[at : at + 64, cols] = split(value)
-
     ladder_sums(3)
     z_recv[z] = z_send[z]
+
+    @pl.loop(1, 16)
+    def _(r):
+        a_copy(r).wait_recv()
+
+    for r in range(4):
+        for w in range(2):
+            pieces = []
+            for q in range(8 * w, 8 * w + 8):
+                k, u = q // tiles, q % tiles
+                if k < 4:
+                    pieces.append(a2a_recv[u, pl.ds(64 * r + k, 16, stride=4), :])
+                else:
+                    pieces.append(jnp.zeros((16, 128), f32))
+            cols = slice(128 * w, 128 * w + 128)
+            for a, value in enumerate(spread(pieces)):
+                at = slice(64 * a + 16 * r, 64 * a + 16 * r + 16)
+                lhs_hi[at, cols], lhs_lo[at, cols] = split(value)
 
     jb_label = [
         occ_label(zero + part // 2) ^ vir_label(lane + 128 * (part % 2)) for part in range(4)
@@ -458,41 +514,47 @@
         z_arrival(r).wait_send()
 
 
-def folded_path(amplitudes, ladder_ints, cycle_ints, occ_irrep, vir_irrep):
+def folded_path(tiles, amplitudes, ladder_ints, cycle_ints, occ_irrep, vir_irrep):
     f32, bf16 = jnp.float32, jnp.bfloat16
     vmem = pltpu.VMEM
     dma = pltpu.SemaphoreType.DMA
-    ladder, cycle = pl.pallas_call(
-        folded_kernel,
+    ladder, cycle, longest = pl.pallas_call(
+        functools.partial(folded_kernel, tiles),
         out_shape=(
             jax.ShapeDtypeStruct((32, 256), f32),
             jax.ShapeDtypeStruct((4, 8, 512), f32),
+            jax.ShapeDtypeStruct((1, 1), jnp.int32),
         ),
         in_specs=[pl.BlockSpec(memory_space=pl.ANY)] * 5,
-        out_specs=[pl.BlockSpec(memory_space=pltpu.VMEM)] * 2,
+        out_specs=[pl.BlockSpec(memory_space=pltpu.VMEM)] * 2 + [pl.BlockSpec(memory_space=pltpu.SMEM)],
         scratch_shapes=[
             vmem((1, 64), jnp.int32), vmem((1, 256), jnp.int32),
             vmem((256, 2048), f32), vmem((64, 2048), f32), vmem((1024, 512), f32),
-            vmem((256, 512), f32), vmem((256, 512), bf16), vmem((256, 512), bf16),
-            vmem((16, 4, 16, 128), f32), vmem((4, 256, 128), f32),
-            vmem((256, 512), bf16), vmem((256, 512), bf16), vmem((16, 64, 512), f32),
+            vmem((256, 128 * tiles), f32), vmem((256, 128 * tiles), bf16), vmem((256, 128 * tiles), bf16),
+            vmem((16, tiles, 16, 128), f32), vmem((tiles, 256, 128), f32),
+            vmem((256, 512), bf16), vmem((256, 512), bf16), vmem((16, 64, 128 * tiles), f32),
             vmem((2, 4, 32, 256), f32), vmem((4, 32, 256), f32), vmem((16, 8, 256), f32), vmem((16, 8, 256), f32),
             vmem((4, 8, 256), f32), vmem((512, 256), bf16), vmem((512, 256), bf16),
             vmem((512, 128), f32), vmem((16, 1, 32, 128), f32), vmem((16, 32, 128), f32), vmem((4, 32, 128), f32),
             dma((5,)), dma((17,)), dma((17,)), dma((16,)), dma((16,)), dma((4,)), dma((4,)),
             dma((16,)), dma((16,)), dma((4,)), dma((4,)), dma((16,)), dma((16,)),
+            pltpu.SemaphoreType.REGULAR, pltpu.SemaphoreType.REGULAR,
         ],
         compiler_params=pltpu.CompilerParams(
-            collective_id=0, has_side_effects=True, vmem_limit_bytes=40 * 1024 * 1024
+            collective_id=0, has_side_effects=True, vmem_limit_bytes=56 * 1024 * 1024
         ),
         cost_estimate=pl.CostEstimate(flops=400_000_000, bytes_accessed=5_000_000, transcendentals=0),
     )(occ_irrep.reshape(1, -1), vir_irrep.reshape(1, -1), amplitudes, ladder_ints.T, cycle_ints)
-    return ladder.T, cycle
+    return ladder.T, cycle, longest[0, 0]
 
 
 def per_device(amplitudes, ladder_ints, cycle_ints, occ_irrep, vir_irrep):
-    fits = jnp.all(vir_irrep[FOLD:] != vir_irrep[:-FOLD])
-    return lax.cond(fits, folded_path, dense_path, amplitudes, ladder_ints, cycle_ints, occ_irrep, vir_irrep)
+    ladder, cycle, longest = folded_path(TILES, amplitudes, ladder_ints, cycle_ints, occ_irrep, vir_irrep)
+    return lax.cond(
+        longest <= 16 * TILES,
+        lambda: (ladder, cycle),
+        lambda: dense_path(amplitudes, ladder_ints, cycle_ints, occ_irrep, vir_irrep),
+    )
 
 
 def solution(mesh):

time: 53.2 us -> 48.5 us (0.912); the launches traced: 52.3 us -> 48.4 us
  Pallas kernels: 48.1 us -> 45.5 us
  other arithmetic: 1.46 us -> 0 us
    pallas_call x1, Pallas kernels: 48.1 us -> 45.5 us  [folded_path(): pl.pallas_call(functools.partial(folded_kernel, tiles), out_shape=(jax.Sh...]
    reduce_and x1 -> x0, other arithmetic: 1.46 us -> none  [per_device(): fits = jnp.all(vir_irrep[FOLD:] != vir_irrep[:-FOLD])]
    unnamed x2 -> x10, local copies, waits for them, and re-layouts: 1.25 us -> 1.26 us
where the time goes in v3:
time: 48.5 us; the launch traced here: 48.4 us
  Pallas kernels  45.5 us (94%)
  between operations  1.39 us (3%)
  local copies, waits for them, and re-layouts  1.26 us (3%)
    pallas_call x1, Pallas kernels, folded_path(): pl.pallas_call(functools.partial(folded_kernel, tiles), out_shape=(jax.Sh...  45.5 us
    unnamed x10, local copies, waits for them, and re-layouts  1.26 us

profile of v3, /device:TPU:6, one launch (start us, length us, event | category | flops | bytes accessed | tf_op | source)
XLA Modules:
  0.0 48.4 jit_solution(18168400501432533355)
XLA Ops:
  0.6 0.0 copy-start
  0.6 0.0 copy-start.1
  0.7 0.0 copy-start.2
  0.7 0.0 copy-start.3
  0.7 45.5 %shard_map.72 = (f32[32,256]{1,0:T(8,128)S(1)}, f32[4,8,512]{2,1,0:T(8,128)S(1)}, s32[1,1]{1,0:T(1,128)}) custom-call(s32[1,64]{1,0:T(1,128)} %bitcast.64, s32[1,256]{1,0:T(1,128)} %bitcast.59, f32[256,2048]{1,0:T(8,128)} %amp_hbm.1, f32[64,2048]{1,0:T(8,128)} %bitcast.57, f32[1024,512]{1,0:T(8,128)} %cyc_hbm.1), custom_call_target="tpu_custom_call" | custom-call | flops 400000000 | bytes 5000000 | tf_op jit(solution)/shard_map/pallas_call | solution.py:521
  46.9 0.0 copy-done
  46.9 0.0 copy-done.1
  46.9 0.0 copy-done.2
  46.9 0.0 copy-done.3
  46.9 0.2 conditional.1
  47.2 0.6 %copy.36 = f32[256,32]{0,1:T(8,128)} copy(f32[256,32]{0,1:T(8,128)S(1)} %get-tuple-element.41) | data formatting | bytes 65536
  47.8 0.6 %copy.37 = f32[4,8,512]{2,1,0:T(8,128)} copy(f32[4,8,512]{2,1,0:T(8,128)S(1)} %get-tuple-element.42) | data formatting | bytes 131072
Async XLA Ops:
  0.6 46.3 %copy-start = (f32[256,2048]{1,0:T(8,128)S(1)}, f32[256,2048]{1,0:T(8,128)}, u32[]{:S(2)}) copy-start(f32[256,2048]{1,0:T(8,128)} %amp_hbm.1) | copy-start | bytes 6291460
  0.6 46.3 %copy-start.1 = (f32[2048,64]{0,1:T(8,128)S(1)}, f32[2048,64]{0,1:T(8,128)}, u32[]{:S(2)}) copy-start(f32[2048,64]{0,1:T(8,128)} %param.8) | copy-start | bytes 1572868
  0.7 46.3 %copy-start.2 = (s32[256]{0:T(256)S(1)}, s32[256]{0:T(256)}, u32[]{:S(2)}) copy-start(s32[256]{0:T(256)} %param.11) | copy-start | bytes 3076
  0.7 46.3 %copy-start.3 = (s32[64]{0:T(128)S(1)}, s32[64]{0:T(128)}, u32[]{:S(2)}) copy-start(s32[64]{0:T(128)} %param.10) | copy-start | bytes 772

commit v4 on v3

--- a/solution.py
+++ b/solution.py
@@ -246,7 +246,6 @@
             amp_fold[rows, cols] = folded
             amp_hi[rows, cols], amp_lo[rows, cols] = split(folded)
 
-    regroup(amp_fold, a2a_send, 4)
     got(0)
     go(4, 5, 6)
     got(1)
@@ -254,6 +253,7 @@
     got(2)
     go(8, 12)
 
+    regroup(amp_fold, a2a_send, 4)
     mine16 = pl.ds(pl.multiple_of(16 * g, 16), 16)
 
     def a_copy(r):
@@ -262,12 +262,6 @@
             src_ref=a2a_send.at[to], dst_ref=a2a_recv.at[:, mine16],
             send_sem=a_ss.at[r], recv_sem=a_rs.at[r], device_id=(to, s), device_id_type=MESH,
         )
-
-    @pl.loop(1, 16)
-    def _(r):
-        a_copy(r).start()
-
-    a2a_recv[:, mine16, :] = a2a_send[g]
 
     load_o.wait()
     load_v.wait()
@@ -383,6 +377,12 @@
     ladder_product(1)
     got(9, 10)
     go(16)
+
+    @pl.loop(1, 16)
+    def _(r):
+        a_copy(r).start()
+
+    a2a_recv[:, mine16, :] = a2a_send[g]
 
     ladder_sums(0)
     got(12, 15)
@@ -541,7 +541,7 @@
             pltpu.SemaphoreType.REGULAR, pltpu.SemaphoreType.REGULAR,
         ],
         compiler_params=pltpu.CompilerParams(
-            collective_id=0, has_side_effects=True, vmem_limit_bytes=56 * 1024 * 1024
+            collective_id=0, has_side_effects=True, vmem_limit_bytes=62 * 1024 * 1024
         ),
         cost_estimate=pl.CostEstimate(flops=400_000_000, bytes_accessed=5_000_000, transcendentals=0),
     )(occ_irrep.reshape(1, -1), vir_irrep.reshape(1, -1), amplitudes, ladder_ints.T, cycle_ints)

time: 48.5 us -> 48 us (0.990)
  Pallas kernels: 45.5 us -> 45 us
    pallas_call x1, Pallas kernels: 45.5 us -> 45 us  [folded_path(): pl.pallas_call(functools.partial(folded_kernel, tiles), out_shape=(jax.Sh...]
    unnamed x10 -> x8, local copies, waits for them, and re-layouts: 1.26 us -> 1.26 us
where the time goes in v4:
time: 48 us; the launch traced here: 47.9 us
  Pallas kernels  45 us (94%)
  between operations  1.38 us (3%)
  local copies, waits for them, and re-layouts  1.26 us (3%)
    pallas_call x1, Pallas kernels, folded_path(): pl.pallas_call(functools.partial(folded_kernel, tiles), out_shape=(jax.Sh...  45 us
    unnamed x8, local copies, waits for them, and re-layouts  1.26 us

profile of v4, /device:TPU:6, one launch (start us, length us, event | category | flops | bytes accessed | tf_op | source)
XLA Modules:
  0.0 47.9 jit_solution(6723285217501435351)
XLA Ops:
  0.6 0.0 copy-start.1
  0.6 0.0 copy-start.2
  0.7 0.0 copy-start.3
  0.7 45.0 %shard_map.72 = (f32[32,256]{1,0:T(8,128)S(1)}, f32[4,8,512]{2,1,0:T(8,128)S(1)}, s32[1,1]{1,0:T(1,128)}) custom-call(s32[1,64]{1,0:T(1,128)} %bitcast.64, s32[1,256]{1,0:T(1,128)} %bitcast.59, f32[256,2048]{1,0:T(8,128)} %amp_hbm.1, f32[64,2048]{1,0:T(8,128)} %bitcast.57, f32[1024,512]{1,0:T(8,128)} %cyc_hbm.1), custom_call_target="tpu_custom_call" | custom-call | flops 400000000 | bytes 5000000 | tf_op jit(solution)/shard_map/pallas_call | solution.py:521
  46.4 0.0 copy-done.1
  46.4 0.0 copy-done.2
  46.4 0.0 copy-done.3
  46.4 0.2 conditional.1
  46.6 0.6 %copy.36 = f32[256,32]{0,1:T(8,128)} copy(f32[256,32]{0,1:T(8,128)S(1)} %get-tuple-element.41) | data formatting | bytes 65536
  47.2 0.6 %copy.37 = f32[4,8,512]{2,1,0:T(8,128)} copy(f32[4,8,512]{2,1,0:T(8,128)S(1)} %get-tuple-element.42) | data formatting | bytes 131072
Async XLA Ops:
  0.6 45.7 %copy-start.1 = (f32[2048,64]{0,1:T(8,128)S(1)}, f32[2048,64]{0,1:T(8,128)}, u32[]{:S(2)}) copy-start(f32[2048,64]{0,1:T(8,128)} %param.8) | copy-start | bytes 1572868
  0.6 45.7 %copy-start.2 = (s32[256]{0:T(256)S(1)}, s32[256]{0:T(256)}, u32[]{:S(2)}) copy-start(s32[256]{0:T(256)} %param.11) | copy-start | bytes 3076
  0.7 45.7 %copy-start.3 = (s32[64]{0:T(128)S(1)}, s32[64]{0:T(128)}, u32[]{:S(2)}) copy-start(s32[64]{0:T(128)} %param.10) | copy-start | bytes 772

commit v5 on v4

--- a/solution.py
+++ b/solution.py
@@ -107,7 +107,6 @@
     load_o.start()
     load_v.start()
     load_a.start()
-    load_w.start()
 
     barrier = pltpu.get_barrier_semaphore()
 
@@ -237,6 +236,7 @@
     go(0, 1, 2, 3)
 
     load_a.wait()
+    load_w.start()
 
     @pl.loop(0, 16)
     def _(r):

time: 48 us -> 47.8 us (level)
  no operation moved by 1% of the time
where the time goes in v5:
time: 47.8 us; the launch traced here: 47.6 us
  Pallas kernels  44.7 us (94%)
  between operations  1.38 us (3%)
  local copies, waits for them, and re-layouts  1.26 us (3%)
    pallas_call x1, Pallas kernels, folded_path(): pl.pallas_call(functools.partial(folded_kernel, tiles), out_shape=(jax.Sh...  44.7 us
    unnamed x8, local copies, waits for them, and re-layouts  1.26 us

profile of v5, /device:TPU:6, one launch (start us, length us, event | category | flops | bytes accessed | tf_op | source)
XLA Modules:
  0.0 47.6 jit_solution(14715020643279439627)
XLA Ops:
  0.6 0.0 copy-start.1
  0.6 0.0 copy-start.2
  0.7 0.0 copy-start.3
  0.7 44.7 %shard_map.72 = (f32[32,256]{1,0:T(8,128)S(1)}, f32[4,8,512]{2,1,0:T(8,128)S(1)}, s32[1,1]{1,0:T(1,128)}) custom-call(s32[1,64]{1,0:T(1,128)} %bitcast.64, s32[1,256]{1,0:T(1,128)} %bitcast.59, f32[256,2048]{1,0:T(8,128)} %amp_hbm.1, f32[64,2048]{1,0:T(8,128)} %bitcast.57, f32[1024,512]{1,0:T(8,128)} %cyc_hbm.1), custom_call_target="tpu_custom_call" | custom-call | flops 400000000 | bytes 5000000 | tf_op jit(solution)/shard_map/pallas_call | solution.py:521
  46.1 0.0 copy-done.1
  46.1 0.0 copy-done.2
  46.1 0.0 copy-done.3
  46.1 0.2 conditional.1
  46.3 0.6 %copy.36 = f32[256,32]{0,1:T(8,128)} copy(f32[256,32]{0,1:T(8,128)S(1)} %get-tuple-element.41) | data formatting | bytes 65536
  46.9 0.6 %copy.37 = f32[4,8,512]{2,1,0:T(8,128)} copy(f32[4,8,512]{2,1,0:T(8,128)S(1)} %get-tuple-element.42) | data formatting | bytes 131072
Async XLA Ops:
  0.6 45.4 %copy-start.1 = (f32[2048,64]{0,1:T(8,128)S(1)}, f32[2048,64]{0,1:T(8,128)}, u32[]{:S(2)}) copy-start(f32[2048,64]{0,1:T(8,128)} %param.8) | copy-start | bytes 1572868
  0.6 45.4 %copy-start.2 = (s32[256]{0:T(256)S(1)}, s32[256]{0:T(256)}, u32[]{:S(2)}) copy-start(s32[256]{0:T(256)} %param.11) | copy-start | bytes 3076
  0.7 45.4 %copy-start.3 = (s32[64]{0:T(128)S(1)}, s32[64]{0:T(128)}, u32[]{:S(2)}) copy-start(s32[64]{0:T(128)} %param.10) | copy-start | bytes 772
